TPU v7x, 512 devices: a whole 4x4x16 slice. The times are simulated.
512 devices in a mesh: node: 8 (over y, core), scen: 64 (over z, x).
Axes of the slice: x: 4, y: 4, z: 16, core: 2. Of those that a mesh axis runs over, the one named last changes fastest.
Arguments:
- sample_submatrices: bfloat16 [8192, 128, 1024], P(('node', 'scen')), may hold values from -0.176776695 to 0.176776695
- penalty_weights: float32 [8192, 128], P(('node', 'scen')), may hold values from 0.001 to 10
- sample_patch_pattern: int32 [8192, 8], P(('node', 'scen')), may hold values 0 or 1
- terminal_penalty_entries: float32 [8, 1024], P('node'), may hold values from 0.25 to 4
- terminal_ancestor_coupler: bfloat16 [8, 1024, 256], P('node'), may hold values from -0.1875 to 0.1875
- secondary_penalty_entries: float32 [2, 256], replicated, may hold values from 0.25 to 4
- secondary_base_coupler: bfloat16 [2, 256, 128], replicated, may hold values from -0.375 to 0.375
- opening_penalty_entries: float32 [128], replicated, may hold values from 0.25 to 4
Outputs:
- node_factor: float32 [8, 1024, 1024], P('node', 'scen')
- parent_factor: float32 [2, 256, 256], replicated
- root_factor: float32 [128, 128], replicated
All inputs are finite; a program needn't handle non-finite values. No bound on the sum of `sample_patch_pattern` on one device may be relied on, other than what follows from the above.
Results may differ from a plain program's by a relative error of at most 0.00037.
Values sent between devices are 32-bit elements; how exact they have to be, the bound alone decides.
No kernel may reach another device: no remote copies, remote signals or barrier semaphores. Data moves between devices by JAX's collectives and lax.ppermute only.
A program may use at most 128 MiB of HBM per device.

v0:
```python
import jax
import jax.numpy as jnp
from jax import lax
from jax.sharding import PartitionSpec as P

PARENTS = 2


def column_mask(sample_patch_pattern, width):
    tiles = sample_patch_pattern.shape[1]
    size = width // tiles
    owner = lax.broadcasted_iota(jnp.int32, (tiles, width), 1) // size
    table = (owner == lax.broadcasted_iota(jnp.int32, (tiles, width), 0)).astype(jnp.float32)
    return jnp.dot(sample_patch_pattern.astype(jnp.float32), table, precision=lax.Precision.HIGHEST)


def per_device(
    sample_submatrices,
    penalty_weights,
    sample_patch_pattern,
    terminal_penalty_entries,
    terminal_ancestor_coupler,
    secondary_penalty_entries,
    secondary_base_coupler,
    opening_penalty_entries,
):
    width = sample_submatrices.shape[2]
    patch_field_pattern = column_mask(sample_patch_pattern, width)
    midpoint_extent = (
        sample_submatrices.astype(jnp.float32)
        * jnp.sqrt(penalty_weights)[:, :, None]
        * patch_field_pattern[:, None, :]
    )
    midpoint_extent = midpoint_extent.astype(jnp.bfloat16).reshape(-1, width)
    share_rows = width // lax.axis_size("scen")
    whole_term = lax.dot_general(
        midpoint_extent,
        midpoint_extent,
        (((0,), (0,)), ((), ())),
        preferred_element_type=jnp.float32,
    )
    schur = lax.psum(whole_term, "scen")
    block = schur + jnp.diag(terminal_penalty_entries[0])
    factor = jnp.linalg.cholesky(block)
    first_row = lax.axis_index("scen") * share_rows
    own_rows = lax.dynamic_slice_in_dim(factor, first_row, share_rows, 0)[None]
    reduced = jax.scipy.linalg.solve_triangular(
        factor, terminal_ancestor_coupler[0].astype(jnp.float32), lower=True
    )
    condensed = jnp.dot(reduced.T, reduced, precision=lax.Precision.HIGHEST)
    node_count = lax.axis_size("node")
    parent_ids = jnp.arange(PARENTS, dtype=jnp.int32)
    my_parent = lax.axis_index("node") * PARENTS // node_count
    selector = (parent_ids == my_parent).astype(jnp.float32)
    sums = lax.psum(selector[:, None, None] * condensed[None], "node")
    parent_block = sums + jax.vmap(jnp.diag)(secondary_penalty_entries)
    parent_factor = jnp.linalg.cholesky(parent_block)
    solve_one = lambda fac, rhs: jax.scipy.linalg.solve_triangular(fac, rhs, lower=True)
    parent_reduced = jax.vmap(solve_one)(parent_factor, secondary_base_coupler.astype(jnp.float32))
    pieces = jnp.einsum(
        "bpr,bps->rs", parent_reduced, parent_reduced, precision=lax.Precision.HIGHEST
    )
    root_block = jnp.diag(opening_penalty_entries) + pieces
    root_factor = jnp.linalg.cholesky(root_block)
    return (own_rows, parent_factor, root_factor)


def solution(mesh):
    placed = (
        P(("node", "scen"), None, None),
        P(("node", "scen"), None),
        P(("node", "scen"), None),
        P("node", None),
        P("node", None, None),
        P(),
        P(),
        P(),
    )
    return jax.shard_map(
        per_device,
        mesh=mesh,
        in_specs=placed,
        out_specs=(P("node", "scen", None), P(), P()),
        check_vma=False,
    )
```

profile of v0, /device:TPU:2, one launch (start us, length us, event | category | flops | bytes accessed | tf_op | source)
XLA Modules:
  0.0 879.4 jit_solution(12251882770582183225)
XLA Ops:
  8.9 10.5 %fusion.5 = f32[1024,1024]{0,1:T(8,128)} fusion(bf16[16,128,1024]{2,1,0:T(8,128)(2,1)} %param.8, f32[16,1024]{1,0:T(8,128)S(1)} %convolution_bitcast_fusion, f32[16,128]{1,0:T(8,128)S(1)} %sqrt.3), kind=kOutput, calls=%fused_computation.16 | convolution fusion | flops 4303355904 | bytes 8462336 | tf_op jit(solution)/shard_map/dot_general | solution.py:36
  20.6 292.1 %all-reduce.5.cloned.1.call-done = f32[1024,1024]{0,1:T(8,128)} async-done(((f32[1024,1024]{0,1:T(8,128)}), f32[1024,1024]{0,1:T(8,128)}) %all-reduce.5.cloned.1.call-update) | async-done | bytes 4194320 | tf_op jit(solution)/shard_map/psum | solution.py:42
  312.7 4.8 select_add_fusion
  317.5 5.5 copy.78
  323.0 4.4 fusion.1
  327.5 1.9 copy-done.1
  329.4 11.7 %cholesky.285 = f32[128,128]{1,0:T(8,128)S(1)} custom-call(f32[128,128]{1,0:T(8,128)S(1)} %cholesky.740), custom_call_target="Cholesky" | custom-call | tf_op jit(solution)/shard_map/jit(cholesky)/cholesky | solution.py:44
  341.3 9.8 %custom-call.83 = f32[1,128,128]{1,2,0:T(8,128)S(1)} custom-call(f32[1,128,128]{2,1,0:T(8,128)S(1)} %get-tuple-element.116), custom_call_target="InvertDiagBlocksLowerTriangular" | custom-call | tf_op jit(solution)/shard_map/jit(cholesky)/cholesky | solution.py:44
  351.1 1.5 fusion.21
  352.8 1.6 convolution_subtract_fusion
  354.4 11.7 %cholesky.308 = f32[128,128]{1,0:T(8,128)S(1)} custom-call(f32[128,128]{1,0:T(8,128)S(1)} %cholesky.744), custom_call_target="Cholesky" | custom-call | tf_op jit(solution)/shard_map/jit(cholesky)/cholesky | solution.py:44
  366.5 9.8 %custom-call.84 = f32[1,128,128]{1,2,0:T(8,128)S(1)} custom-call(f32[1,128,128]{2,1,0:T(8,128)S(1)} %get-tuple-element.114), custom_call_target="InvertDiagBlocksLowerTriangular" | custom-call | tf_op jit(solution)/shard_map/jit(cholesky)/cholesky | solution.py:44
  377.4 2.0 copy-done
  379.4 2.4 convolution_subtract_fusion.1
  381.8 11.7 %cholesky.335 = f32[128,128]{1,0:T(8,128)S(1)} custom-call(f32[128,128]{1,0:T(8,128)S(1)} %cholesky.749), custom_call_target="Cholesky" | custom-call | tf_op jit(solution)/shard_map/jit(cholesky)/cholesky | solution.py:44
  394.3 9.8 %custom-call.85 = f32[1,128,128]{1,2,0:T(8,128)S(1)} custom-call(f32[1,128,128]{2,1,0:T(8,128)S(1)} %get-tuple-element.112), custom_call_target="InvertDiagBlocksLowerTriangular" | custom-call | tf_op jit(solution)/shard_map/jit(cholesky)/cholesky | solution.py:44
  404.1 1.2 convolution_dynamic-update-slice_fusion.1
  405.3 3.5 convolution_subtract_fusion.2
  408.9 11.7 %cholesky.612 = f32[128,128]{1,0:T(8,128)S(1)} custom-call(f32[128,128]{1,0:T(8,128)S(1)} %cholesky.754), custom_call_target="Cholesky" | custom-call | tf_op jit(solution)/shard_map/jit(cholesky)/cholesky | solution.py:44
  421.4 9.8 %custom-call.86 = f32[1,128,128]{1,2,0:T(8,128)S(1)} custom-call(f32[1,128,128]{2,1,0:T(8,128)S(1)} %get-tuple-element.110), custom_call_target="InvertDiagBlocksLowerTriangular" | custom-call | tf_op jit(solution)/shard_map/jit(cholesky)/cholesky | solution.py:44
  431.2 1.1 convolution_dynamic-update-slice_fusion.2
  432.3 3.2 convolution_subtract_fusion.3
  435.5 11.9 %cholesky.631 = f32[128,128]{1,0:T(8,128)S(1)} custom-call(f32[128,128]{1,0:T(8,128)S(1)} %cholesky.759), custom_call_target="Cholesky" | custom-call | tf_op jit(solution)/shard_map/jit(cholesky)/cholesky | solution.py:44
  448.1 9.8 %custom-call.87 = f32[1,128,128]{1,2,0:T(8,128)S(1)} custom-call(f32[1,128,128]{2,1,0:T(8,128)S(1)} %get-tuple-element.108), custom_call_target="InvertDiagBlocksLowerTriangular" | custom-call | tf_op jit(solution)/shard_map/jit(cholesky)/cholesky | solution.py:44
  457.9 1.1 convolution_dynamic-update-slice_fusion.3
  459.1 3.2 convolution_subtract_fusion.4
  462.3 11.7 %cholesky.651 = f32[128,128]{1,0:T(8,128)S(1)} custom-call(f32[128,128]{1,0:T(8,128)S(1)} %cholesky.764), custom_call_target="Cholesky" | custom-call | tf_op jit(solution)/shard_map/jit(cholesky)/cholesky | solution.py:44
  474.8 9.8 %custom-call.88 = f32[1,128,128]{1,2,0:T(8,128)S(1)} custom-call(f32[1,128,128]{2,1,0:T(8,128)S(1)} %get-tuple-element.106), custom_call_target="InvertDiagBlocksLowerTriangular" | custom-call | tf_op jit(solution)/shard_map/jit(cholesky)/cholesky | solution.py:44
  485.6 2.9 convolution_subtract_fusion.11
  488.5 11.7 %cholesky.671 = f32[128,128]{1,0:T(8,128)S(1)} custom-call(f32[128,128]{1,0:T(8,128)S(1)} %cholesky.769), custom_call_target="Cholesky" | custom-call | tf_op jit(solution)/shard_map/jit(cholesky)/cholesky | solution.py:44
  501.0 9.8 %custom-call.89 = f32[1,128,128]{1,2,0:T(8,128)S(1)} custom-call(f32[1,128,128]{2,1,0:T(8,128)S(1)} %get-tuple-element.104), custom_call_target="InvertDiagBlocksLowerTriangular" | custom-call | tf_op jit(solution)/shard_map/jit(cholesky)/cholesky | solution.py:44
  511.8 2.2 convolution_subtract_fusion.15
  514.0 11.7 %cholesky.689 = f32[128,128]{1,0:T(8,128)S(1)} custom-call(f32[128,128]{1,0:T(8,128)S(1)} %convolution_subtract_fusion.15), custom_call_target="Cholesky" | custom-call | tf_op jit(solution)/shard_map/jit(cholesky)/cholesky | solution.py:44
  536.8 6.6 fusion.4
  543.4 29.3 %while.2 = (s32[]{:T(128)}, f32[1024,1024]{0,1:T(8,128)}, s32[8,2]{0,1:T(2,128)S(1)}, f32[8,128,128]{2,1,0:T(8,128)}, s32[]{:T(128)}) while((s32[]{:T(128)}, f32[1024,1024]{0,1:T(8,128)}, s32[8,2]{0,1:T(2,128)S(1)}, f32[8,128,128]{2,1,0:T(8,128)}, s32[]{:T(128)}) %tuple.79), condition=%wide.while_cond, body=%wide.while_body.sunk | while | flops 2 | bytes 393329 | solution.py:47
  544.4 2.3 dynamic-slice.15
  548.0 2.3 dynamic-slice.15
  551.6 2.3 dynamic-slice.15
  555.3 2.3 dynamic-slice.15
  558.9 2.3 dynamic-slice.15
  562.5 2.3 dynamic-slice.15
  566.1 2.3 dynamic-slice.15
  569.8 2.2 dynamic-slice.15
  572.7 79.4 %custom-call.90 = f32[8,128,128]{1,2,0:T(8,128)S(1)} custom-call(f32[8,128,128]{2,1,0:T(8,128)} %get-tuple-element.10), custom_call_target="InvertDiagBlocksLowerTriangular" | custom-call | tf_op jit(solution)/shard_map/jit(_solve_triangular)/triangular_solve | solution.py:47
  652.4 1.2 convolution_subtract_fusion.10
  653.9 1.3 convolution_subtract_fusion.8
  655.6 1.4 convolution_subtract_fusion.7
  657.3 1.6 convolution_subtract_fusion.6
  659.2 1.7 convolution_subtract_fusion.5
  661.2 1.8 convolution_subtract_fusion.9
  663.4 2.0 convolution_subtract_fusion.14
  665.7 1.8 fusion.90
  668.5 1.2 constant_dynamic-slice_fusion.3
  670.5 70.3 %all-reduce.7.cloned.1.call-done = f32[2,256,256]{1,2,0:T(8,128)} async-done(((f32[2,256,256]{1,2,0:T(8,128)}), f32[2,256,256]{1,2,0:T(8,128)}) %all-reduce.7.cloned.1.call-update) | async-done | bytes 524304 | tf_op jit(solution)/shard_map/psum | solution.py:55
  742.1 1.1 fusion.18
  743.3 23.6 %custom-call.91 = f32[2,128,128]{2,1,0:T(8,128)S(1)} custom-call(f32[2,128,128]{2,1,0:T(8,128)S(1)} %cholesky.773), custom_call_target="Cholesky" | custom-call | tf_op jit(solution)/shard_map/jit(cholesky)/cholesky | solution.py:57
  767.0 19.7 %custom-call.92 = f32[2,1,128,128]{2,3,1,0:T(8,128)S(1)} custom-call(f32[2,1,128,128]{3,2,1,0:T(8,128)S(1)} %select_bitcast_fusion), custom_call_target="InvertDiagBlocksLowerTriangular" | custom-call | tf_op jit(solution)/shard_map/jit(cholesky)/cholesky | solution.py:57
  787.6 23.5 %custom-call.93 = f32[2,128,128]{2,1,0:T(8,128)S(1)} custom-call(f32[2,128,128]{2,1,0:T(8,128)S(1)} %convolution_subtract_fusion.13), custom_call_target="Cholesky" | custom-call | tf_op jit(solution)/shard_map/jit(cholesky)/cholesky | solution.py:57
  812.7 4.4 while.3
  813.3 1.4 constant_dynamic-slice_fusion.9
  815.5 1.4 constant_dynamic-slice_fusion.9
  817.1 39.5 %custom-call.94 = f32[2,2,128,128]{2,3,1,0:T(8,128)S(1)} custom-call(f32[2,2,128,128]{3,2,1,0:T(8,128)S(1)} %bitcast.185), custom_call_target="InvertDiagBlocksLowerTriangular" | custom-call | tf_op jit(solution)/shard_map/vmap(jit(_solve_triangular))/triangular_solve | solution.py:58
  858.5 11.7 %cholesky.729 = f32[128,128]{1,0:T(8,128)S(1)} custom-call(f32[128,128]{1,0:T(8,128)S(1)} %fusion.66), custom_call_target="Cholesky" | custom-call | tf_op jit(solution)/shard_map/jit(cholesky)/cholesky | solution.py:64
  871.0 1.3 select_select_fusion.2
  (152 shorter events, 38.9 us)
Async XLA Ops:
  7.2 305.5 %all-reduce.5.cloned.1.call-start = ((), (), s32[]{:S(2)}) async-start(), calls=%async_computation | async-start | bytes 8388608 | tf_op jit(solution)/shard_map/psum | solution.py:42
  19.3 1.0 copy-start.2
  19.3 293.4 %copy-start.4 = (f32[1,1024]{1,0:T(1,128)S(1)}, f32[1,1024]{1,0:T(1,128)}, u32[]{:S(2)}) copy-start(f32[1,1024]{1,0:T(1,128)} %param.11) | copy-start | bytes 12292
  19.4 721.5 %all-reduce.7.cloned.1.call-start = ((), (), s32[]{:S(2)}) async-start(), calls=%async_computation.1 | async-start | bytes 1048576 | tf_op jit(solution)/shard_map/psum | solution.py:55
  327.5 1.9 copy-start.1
  377.4 2.0 copy-start
  663.1 77.8 %copy-start.5 = (f32[2,256]{1,0:T(2,128)S(1)}, f32[2,256]{1,0:T(2,128)}, u32[]{:S(2)}) copy-start(f32[2,256]{1,0:T(2,128)} %param.13) | copy-start | bytes 6148
  787.5 69.1 %copy-start.3 = (bf16[2,256,128]{2,1,0:T(8,128)(2,1)S(1)}, bf16[2,256,128]{2,1,0:T(8,128)(2,1)}, u32[]{:S(2)}) copy-start(bf16[2,256,128]{2,1,0:T(8,128)(2,1)} %param.14) | copy-start | bytes 393220
  811.4 47.0 %copy-start.6 = (f32[128]{0:T(128)S(1)}, f32[128]{0:T(128)}, u32[]{:S(2)}) copy-start(f32[128]{0:T(128)} %param.15) | copy-start | bytes 1540
Sparse Core Ops, SparseCore 0:
  19.5 293.1 all-reduce.4
  668.6 72.2 all-reduce.6
where the time goes:
time: 886 us; the launch traced here: 879 us
  other arithmetic  387 us (44%)
  waiting for transfers between devices  362 us (41%)
  matrix products  55.4 us (6%)
  local copies, waits for them, and re-layouts  53.4 us (6%)
  between operations  20.3 us (2%)
    psum x1, waiting for transfers between devices, per_device(): schur = lax.psum(whole_term, 'scen')  292 us
    another operation x33, other arithmetic, per_device(): factor = jnp.linalg.cholesky(block)  168 us
    another operation x3, other arithmetic, per_device(): jax.scipy.linalg.solve_triangular(factor, terminal_ancestor_coupler[0].as...  86 us
    psum x1, waiting for transfers between devices, per_device(): sums = lax.psum(selector[:, None, None] * condensed[None], 'node')  70.3 us
    another operation x8, other arithmetic, per_device(): parent_factor = jnp.linalg.cholesky(parent_block)  67.1 us
    another operation x3, other arithmetic, per_device(): jax.scipy.linalg.solve_triangular(fac, rhs, lower=True)  39.7 us
    another operation x50, local copies, waits for them, and re-layouts  33.2 us
    another operation x14, matrix products, per_device(): factor = jnp.linalg.cholesky(block)  26.4 us
  transfers between devices with their start and end apart: 2, of which 2 were waited for; matrix products, arithmetic and copies ran while one was open for 0% of the time, Pallas kernels for 0%

commit v1 on v0

--- a/solution.py
+++ b/solution.py
@@ -52,7 +52,7 @@
     parent_ids = jnp.arange(PARENTS, dtype=jnp.int32)
     my_parent = lax.axis_index("node") * PARENTS // node_count
     selector = (parent_ids == my_parent).astype(jnp.float32)
-    sums = lax.psum(selector[:, None, None] * condensed[None], "node")
+    sums = jnp.sum(lax.all_gather(selector[:, None, None] * condensed[None], "node"), axis=0)
     parent_block = sums + jax.vmap(jnp.diag)(secondary_penalty_entries)
     parent_factor = jnp.linalg.cholesky(parent_block)
     solve_one = lambda fac, rhs: jax.scipy.linalg.solve_triangular(fac, rhs, lower=True)

time: 886 us -> 844 us (0.953)
  the two profiles are of different devices: /device:TPU:2 before, /device:TPU:1 now
where the time goes in v1:
time: 844 us; the launch traced here: 838 us
  other arithmetic  388 us (46%)
  waiting for transfers between devices  327 us (39%)
  matrix products  55.2 us (7%)
  local copies, waits for them, and re-layouts  46.9 us (6%)
  between operations  20.3 us (2%)
    psum x1, waiting for transfers between devices, per_device(): schur = lax.psum(whole_term, 'scen')  285 us
    another operation x33, other arithmetic, per_device(): factor = jnp.linalg.cholesky(block)  168 us
    another operation x3, other arithmetic, per_device(): jax.scipy.linalg.solve_triangular(factor, terminal_ancestor_coupler[0].as...  85.2 us
    another operation x8, other arithmetic, per_device(): parent_factor = jnp.linalg.cholesky(parent_block)  67.1 us
    all_gather x1, waiting for transfers between devices, per_device(): lax.all_gather(selector[:, None, None] * condensed[None], 'node')  42.3 us
    another operation x3, other arithmetic, per_device(): jax.scipy.linalg.solve_triangular(fac, rhs, lower=True)  40.5 us
    another operation x46, local copies, waits for them, and re-layouts  27.9 us
    another operation x14, matrix products, per_device(): factor = jnp.linalg.cholesky(block)  26.4 us
  transfers between devices with their start and end apart: 2, of which 2 were waited for; matrix products, arithmetic and copies ran while one was open for 0% of the time, Pallas kernels for 0%

profile of v1, /device:TPU:1, one launch (start us, length us, event | category | flops | bytes accessed | tf_op | source)
XLA Modules:
  0.0 838.2 jit_solution(10633461907529755351)
XLA Ops:
  8.9 10.5 %fusion.5 = f32[1024,1024]{0,1:T(8,128)} fusion(bf16[16,128,1024]{2,1,0:T(8,128)(2,1)} %param.8, f32[16,1024]{1,0:T(8,128)S(1)} %convolution_bitcast_fusion, f32[16,128]{1,0:T(8,128)S(1)} %sqrt.3), kind=kOutput, calls=%fused_computation.15 | convolution fusion | flops 4303355904 | bytes 8462336 | tf_op jit(solution)/shard_map/dot_general | solution.py:36
  20.5 285.0 %all-reduce.4.cloned.1.call-done = f32[1024,1024]{0,1:T(8,128)} async-done(((f32[1024,1024]{0,1:T(8,128)}), f32[1024,1024]{0,1:T(8,128)}) %all-reduce.4.cloned.1.call-update) | async-done | bytes 4194320 | tf_op jit(solution)/shard_map/psum | solution.py:42
  305.5 4.8 select_add_fusion
  310.4 5.5 copy.94
  315.9 4.4 fusion.1
  320.3 1.9 copy-done.1
  322.2 11.7 %cholesky.285 = f32[128,128]{1,0:T(8,128)S(1)} custom-call(f32[128,128]{1,0:T(8,128)S(1)} %cholesky.740), custom_call_target="Cholesky" | custom-call | tf_op jit(solution)/shard_map/jit(cholesky)/cholesky | solution.py:44
  334.1 9.8 %custom-call.83 = f32[1,128,128]{1,2,0:T(8,128)S(1)} custom-call(f32[1,128,128]{2,1,0:T(8,128)S(1)} %get-tuple-element.100), custom_call_target="InvertDiagBlocksLowerTriangular" | custom-call | tf_op jit(solution)/shard_map/jit(cholesky)/cholesky | solution.py:44
  343.9 1.5 fusion.20
  345.6 1.6 convolution_subtract_fusion
  347.2 11.7 %cholesky.308 = f32[128,128]{1,0:T(8,128)S(1)} custom-call(f32[128,128]{1,0:T(8,128)S(1)} %cholesky.744), custom_call_target="Cholesky" | custom-call | tf_op jit(solution)/shard_map/jit(cholesky)/cholesky | solution.py:44
  359.3 9.8 %custom-call.84 = f32[1,128,128]{1,2,0:T(8,128)S(1)} custom-call(f32[1,128,128]{2,1,0:T(8,128)S(1)} %get-tuple-element.98), custom_call_target="InvertDiagBlocksLowerTriangular" | custom-call | tf_op jit(solution)/shard_map/jit(cholesky)/cholesky | solution.py:44
  370.2 2.0 copy-done
  372.2 2.4 convolution_subtract_fusion.1
  374.6 11.7 %cholesky.335 = f32[128,128]{1,0:T(8,128)S(1)} custom-call(f32[128,128]{1,0:T(8,128)S(1)} %cholesky.749), custom_call_target="Cholesky" | custom-call | tf_op jit(solution)/shard_map/jit(cholesky)/cholesky | solution.py:44
  387.1 9.8 %custom-call.85 = f32[1,128,128]{1,2,0:T(8,128)S(1)} custom-call(f32[1,128,128]{2,1,0:T(8,128)S(1)} %get-tuple-element.96), custom_call_target="InvertDiagBlocksLowerTriangular" | custom-call | tf_op jit(solution)/shard_map/jit(cholesky)/cholesky | solution.py:44
  396.9 1.2 convolution_dynamic-update-slice_fusion.1
  398.1 3.5 convolution_subtract_fusion.2
  401.7 11.7 %cholesky.612 = f32[128,128]{1,0:T(8,128)S(1)} custom-call(f32[128,128]{1,0:T(8,128)S(1)} %cholesky.754), custom_call_target="Cholesky" | custom-call | tf_op jit(solution)/shard_map/jit(cholesky)/cholesky | solution.py:44
  414.2 9.8 %custom-call.86 = f32[1,128,128]{1,2,0:T(8,128)S(1)} custom-call(f32[1,128,128]{2,1,0:T(8,128)S(1)} %get-tuple-element.94), custom_call_target="InvertDiagBlocksLowerTriangular" | custom-call | tf_op jit(solution)/shard_map/jit(cholesky)/cholesky | solution.py:44
  424.0 1.1 convolution_dynamic-update-slice_fusion.2
  425.1 3.2 convolution_subtract_fusion.3
  428.3 11.9 %cholesky.631 = f32[128,128]{1,0:T(8,128)S(1)} custom-call(f32[128,128]{1,0:T(8,128)S(1)} %cholesky.759), custom_call_target="Cholesky" | custom-call | tf_op jit(solution)/shard_map/jit(cholesky)/cholesky | solution.py:44
  440.9 9.8 %custom-call.87 = f32[1,128,128]{1,2,0:T(8,128)S(1)} custom-call(f32[1,128,128]{2,1,0:T(8,128)S(1)} %get-tuple-element.92), custom_call_target="InvertDiagBlocksLowerTriangular" | custom-call | tf_op jit(solution)/shard_map/jit(cholesky)/cholesky | solution.py:44
  450.8 1.1 convolution_dynamic-update-slice_fusion.3
  451.9 3.2 convolution_subtract_fusion.4
  455.1 11.7 %cholesky.651 = f32[128,128]{1,0:T(8,128)S(1)} custom-call(f32[128,128]{1,0:T(8,128)S(1)} %cholesky.764), custom_call_target="Cholesky" | custom-call | tf_op jit(solution)/shard_map/jit(cholesky)/cholesky | solution.py:44
  467.6 9.8 %custom-call.88 = f32[1,128,128]{1,2,0:T(8,128)S(1)} custom-call(f32[1,128,128]{2,1,0:T(8,128)S(1)} %get-tuple-element.90), custom_call_target="InvertDiagBlocksLowerTriangular" | custom-call | tf_op jit(solution)/shard_map/jit(cholesky)/cholesky | solution.py:44
  478.4 2.9 convolution_subtract_fusion.11
  481.4 11.7 %cholesky.671 = f32[128,128]{1,0:T(8,128)S(1)} custom-call(f32[128,128]{1,0:T(8,128)S(1)} %cholesky.769), custom_call_target="Cholesky" | custom-call | tf_op jit(solution)/shard_map/jit(cholesky)/cholesky | solution.py:44
  493.8 9.8 %custom-call.89 = f32[1,128,128]{1,2,0:T(8,128)S(1)} custom-call(f32[1,128,128]{2,1,0:T(8,128)S(1)} %get-tuple-element.88), custom_call_target="InvertDiagBlocksLowerTriangular" | custom-call | tf_op jit(solution)/shard_map/jit(cholesky)/cholesky | solution.py:44
  504.6 2.2 convolution_subtract_fusion.15
  506.8 11.7 %cholesky.689 = f32[128,128]{1,0:T(8,128)S(1)} custom-call(f32[128,128]{1,0:T(8,128)S(1)} %convolution_subtract_fusion.15), custom_call_target="Cholesky" | custom-call | tf_op jit(solution)/shard_map/jit(cholesky)/cholesky | solution.py:44
  529.6 6.6 fusion.4
  536.2 24.5 %while.2 = (s32[]{:T(128)}, f32[1024,1024]{0,1:T(8,128)}, s32[8,2]{0,1:T(2,128)S(1)}, f32[8,128,128]{2,1,0:T(8,128)S(1)}, s32[]{:T(128)}) while((s32[]{:T(128)}, f32[1024,1024]{0,1:T(8,128)}, s32[8,2]{0,1:T(2,128)S(1)}, f32[8,128,128]{2,1,0:T(8,128)S(1)}, s32[]{:T(128)}) %tuple.77), condition=%wide.while_cond, body=%wide.while_body.sunk | while | flops 2 | bytes 393329 | solution.py:47
  537.2 2.3 dynamic-slice.15
  540.2 2.3 dynamic-slice.15
  543.3 2.3 dynamic-slice.15
  546.3 2.3 dynamic-slice.15
  549.3 2.3 dynamic-slice.15
  552.3 2.3 dynamic-slice.15
  555.4 2.3 dynamic-slice.15
  558.4 2.2 dynamic-slice.15
  560.7 78.6 %custom-call.90 = f32[8,128,128]{1,2,0:T(8,128)S(1)} custom-call(f32[8,128,128]{2,1,0:T(8,128)S(1)} %get-tuple-element.10), custom_call_target="InvertDiagBlocksLowerTriangular" | custom-call | tf_op jit(solution)/shard_map/jit(_solve_triangular)/triangular_solve | solution.py:47
  639.6 1.2 convolution_subtract_fusion.10
  641.1 1.3 convolution_subtract_fusion.8
  642.7 1.4 convolution_subtract_fusion.7
  644.5 1.6 convolution_subtract_fusion.6
  646.4 1.7 convolution_subtract_fusion.5
  648.4 1.8 convolution_subtract_fusion.9
  650.6 2.0 convolution_subtract_fusion.14
  652.9 1.8 fusion.89
  655.8 1.2 constant_dynamic-slice_fusion.2
  657.8 42.3 %all-gather.2.cloned.1.call-done = f32[8,2,256,256]{3,2,1,0:T(8,128)} async-done(((f32[1,2,256,256]{3,2,1,0:T(8,128)}), f32[8,2,256,256]{3,2,1,0:T(8,128)}) %all-gather.2.cloned.1.call-update) | async-done | bytes 4194320 | tf_op jit(solution)/shard_map/all_gather | solution.py:55
  700.1 2.5 reduce_sum.11
  703.1 23.6 %custom-call.91 = f32[2,128,128]{2,1,0:T(8,128)S(1)} custom-call(f32[2,128,128]{2,1,0:T(8,128)S(1)} %cholesky.773), custom_call_target="Cholesky" | custom-call | tf_op jit(solution)/shard_map/jit(cholesky)/cholesky | solution.py:57
  726.8 19.7 %custom-call.92 = f32[2,1,128,128]{2,3,1,0:T(8,128)S(1)} custom-call(f32[2,1,128,128]{3,2,1,0:T(8,128)S(1)} %select_bitcast_fusion), custom_call_target="InvertDiagBlocksLowerTriangular" | custom-call | tf_op jit(solution)/shard_map/jit(cholesky)/cholesky | solution.py:57
  747.1 23.5 %custom-call.93 = f32[2,128,128]{2,1,0:T(8,128)S(1)} custom-call(f32[2,128,128]{2,1,0:T(8,128)S(1)} %convolution_subtract_fusion.13), custom_call_target="Cholesky" | custom-call | tf_op jit(solution)/shard_map/jit(cholesky)/cholesky | solution.py:57
  771.9 4.1 while.3
  772.5 1.4 bitcast_dynamic-update-slice_fusion.5
  774.6 1.4 bitcast_dynamic-update-slice_fusion.5
  776.0 39.5 %custom-call.94 = f32[2,2,128,128]{2,3,1,0:T(8,128)S(1)} custom-call(f32[2,2,128,128]{3,2,1,0:T(8,128)S(1)} %bitcast.185), custom_call_target="InvertDiagBlocksLowerTriangular" | custom-call | tf_op jit(solution)/shard_map/vmap(jit(_solve_triangular))/triangular_solve | solution.py:58
  817.3 11.7 %cholesky.729 = f32[128,128]{1,0:T(8,128)S(1)} custom-call(f32[128,128]{1,0:T(8,128)S(1)} %fusion.65), custom_call_target="Cholesky" | custom-call | tf_op jit(solution)/shard_map/jit(cholesky)/cholesky | solution.py:64
  829.8 1.3 select_select_fusion.2
  (142 shorter events, 32.1 us)
Async XLA Ops:
  7.2 298.3 %all-reduce.4.cloned.1.call-start = ((), (), s32[]{:S(2)}) async-start(), calls=%async_computation | async-start | bytes 8388608 | tf_op jit(solution)/shard_map/psum | solution.py:42
  19.3 1.0 copy-start.2
  19.3 286.2 %copy-start.4 = (f32[1,1024]{1,0:T(1,128)S(1)}, f32[1,1024]{1,0:T(1,128)}, u32[]{:S(2)}) copy-start(f32[1,1024]{1,0:T(1,128)} %param.11) | copy-start | bytes 12292
  19.4 680.8 %all-gather.2.cloned.1.call-start = ((), (), s32[]{:S(2)}) async-start(), calls=%async_computation.1 | async-start | bytes 4718592 | tf_op jit(solution)/shard_map/all_gather | solution.py:55
  320.3 1.9 copy-start.1
  370.2 2.0 copy-start
  655.6 47.2 %copy-start.5 = (f32[2,256]{1,0:T(2,128)S(1)}, f32[2,256]{1,0:T(2,128)}, u32[]{:S(2)}) copy-start(f32[2,256]{1,0:T(2,128)} %param.13) | copy-start | bytes 6148
  702.6 112.9 %copy-start.3 = (bf16[2,256,128]{2,1,0:T(8,128)(2,1)S(1)}, bf16[2,256,128]{2,1,0:T(8,128)(2,1)}, u32[]{:S(2)}) copy-start(bf16[2,256,128]{2,1,0:T(8,128)(2,1)} %param.14) | copy-start | bytes 393220
  702.9 114.4 %copy-start.6 = (f32[128]{0:T(128)S(1)}, f32[128]{0:T(128)}, u32[]{:S(2)}) copy-start(f32[128]{0:T(128)} %param.15) | copy-start | bytes 1540
Sparse Core Ops, SparseCore 0:
  19.5 285.9 all-reduce.3
  655.8 44.3 all-gather.1
